TPU v7x, 32 devices: a whole 2x2x4 slice. The times are simulated.
32 devices in a mesh: seq: 8 (over y, x, core), tp: 4 (over z).
Axes of the slice: x: 2, y: 2, z: 4, core: 2. Of those that a mesh axis runs over, the one named last changes fastest.
Arguments:
- tokens: bfloat16 [8192, 2048], P('seq'), may hold values from -6 to 6
- doc_start: int32 [8192], P('seq'), may hold values from 0 to 1, as said below
- norm_first: bfloat16 [2048], replicated, may hold values from 0.099609375 to 1.8984375
- in_weight: bfloat16 [2048, 3, 2048], P('seq', None, 'tp'), may hold values from -0.125 to 0.125
- conv_weight: bfloat16 [3, 2048], P(None, 'tp'), may hold values from -3.5 to 3.5
- out_weight: bfloat16 [2048, 2048], P('tp', 'seq'), may hold values from -0.125 to 0.125
- norm_second: bfloat16 [2048], replicated, may hold values from 0.099609375 to 1.8984375
- gate_weight: bfloat16 [2048, 8192], P('seq', 'tp'), may hold values from -0.125 to 0.125
- up_weight: bfloat16 [2048, 8192], P('seq', 'tp'), may hold values from -0.125 to 0.125
- down_weight: bfloat16 [8192, 2048], P('tp', 'seq'), may hold values from -0.125 to 0.125
- out_grad: bfloat16 [8192, 2048], P('seq'), may hold values from -6 to 6
Outputs:
- block_out: bfloat16 [8192, 2048], P('seq')
- tokens_grad: float32 [8192, 2048], P('seq')
- in_grad: float32 [2048, 3, 2048], P('seq', None, 'tp')
- conv_grad: float32 [3, 2048], P(None, 'tp')
- out_proj_grad: float32 [2048, 2048], P('tp', 'seq')
- gate_grad: float32 [2048, 8192], P('seq', 'tp')
- up_grad: float32 [2048, 8192], P('seq', 'tp')
- down_grad: float32 [8192, 2048], P('tp', 'seq')
- norm_first_grad: float32 [2048], replicated
- norm_second_grad: float32 [2048], replicated
Inputs may be any that keep to these rules, and one draw needn't show every extreme that they name: doc_start is 1 at row 0 and wherever a document begins.
All inputs are finite; a program needn't handle non-finite values.
Results may differ from a plain program's by a relative error of at most 0.012.
The roundings to bfloat16 on the way count: a program that leaves them out, or rounds other values in their place, can miss the bound.
Values may be sent and summed in bfloat16 or wider, within the bound.
No kernel may reach another device: no remote copies, remote signals or barrier semaphores. Data moves between devices by JAX's collectives and lax.ppermute only.
A program may use at most 256 MiB of HBM per device.

v0:
```python
import jax
import jax.numpy as jnp
from jax import lax
from jax.sharding import PartitionSpec as P

epsilon = 1e-05


def passed_along(block, axis, distance):
    devices = range(lax.axis_size(axis))
    route = [(i - distance, i) for i in devices if i - distance in devices]
    return lax.ppermute(block, axis, route)


def rms_scale(value):
    return lax.rsqrt(jnp.mean(value * value, axis=1, keepdims=True) + epsilon)


def dot_right(left, right):
    return lax.dot_general(
        left, right, (((1,), (1,)), ((), ())), preferred_element_type=jnp.float32
    )


def dot_left(left, right):
    return lax.dot_general(
        left, right, (((0,), (0,)), ((), ())), preferred_element_type=jnp.float32
    )


def norm_back(grad_normed, scaled, inverse, gain):
    weighted = grad_normed * gain
    back = inverse * (weighted - scaled * jnp.mean(weighted * scaled, axis=1, keepdims=True))
    return (back, jnp.sum(grad_normed * scaled, axis=0))


def local(
    tokens,
    doc_start,
    norm_first,
    in_weight,
    conv_weight,
    out_weight,
    norm_second,
    gate_weight,
    up_weight,
    down_weight,
    out_grad,
):
    in_full, out_full, gate_full, up_full, down_full = (
        lax.all_gather(in_weight, "seq", axis=0, tiled=True),
        lax.all_gather(out_weight, "seq", axis=1, tiled=True),
        lax.all_gather(gate_weight, "seq", axis=0, tiled=True),
        lax.all_gather(up_weight, "seq", axis=0, tiled=True),
        lax.all_gather(down_weight, "seq", axis=1, tiled=True),
    )
    tokens_f = tokens.astype(jnp.float32)
    inverse_one = rms_scale(tokens_f)
    scaled_one = tokens_f * inverse_one
    gain_one = norm_first.astype(jnp.float32)
    normed_one = (scaled_one * gain_one).astype(jnp.bfloat16)
    projected = jnp.einsum(
        "td,dkc->tkc", normed_one, in_full, preferred_element_type=jnp.float32
    ).astype(jnp.bfloat16)
    left_factor = projected[:, 0].astype(jnp.float32)
    out_factor = projected[:, 1].astype(jnp.float32)
    right_factor = projected[:, 2].astype(jnp.float32)
    product = left_factor * right_factor
    kept_one = (1 - doc_start).astype(jnp.float32)[:, None]
    taps = conv_weight.astype(jnp.float32)
    tail_rows = jnp.stack([product[-1], product[-2] * kept_one[-1, 0]])
    before = passed_along(tail_rows, "seq", 1)
    previous = jnp.concatenate([before[:1], product[:-1]], axis=0)
    masked_prev = kept_one * previous
    older = jnp.concatenate([before[1:2], masked_prev[:-1]], axis=0)
    convolved = taps[0] * product + taps[1] * masked_prev + taps[2] * kept_one * older
    gated = (out_factor * convolved).astype(jnp.bfloat16)
    hidden = tokens_f + lax.psum(jnp.dot(gated, out_full, preferred_element_type=jnp.float32), "tp")
    inverse_two = rms_scale(hidden)
    scaled_two = hidden * inverse_two
    gain_two = norm_second.astype(jnp.float32)
    normed_two = (scaled_two * gain_two).astype(jnp.bfloat16)
    gate_val = jnp.dot(normed_two, gate_full, preferred_element_type=jnp.float32)
    up_val = jnp.dot(normed_two, up_full, preferred_element_type=jnp.float32)
    sigma = jax.nn.sigmoid(gate_val)
    swish = gate_val * sigma
    activated = (swish * up_val).astype(jnp.bfloat16)
    ffn_out = lax.psum(jnp.dot(activated, down_full, preferred_element_type=jnp.float32), "tp")
    result = (hidden + ffn_out).astype(jnp.bfloat16)
    grad_act = dot_right(out_grad, down_full)
    down_grad = dot_left(activated, out_grad)
    grad_gate = (grad_act * up_val * sigma * (1.0 + gate_val * (1.0 - sigma))).astype(jnp.bfloat16)
    grad_up = (grad_act * swish).astype(jnp.bfloat16)
    gate_grad = dot_left(normed_two, grad_gate)
    up_grad = dot_left(normed_two, grad_up)
    grad_normed_two = lax.psum(dot_right(grad_gate, gate_full) + dot_right(grad_up, up_full), "tp")
    grad_outside = out_grad.astype(jnp.float32)
    back_two, gain_two_grad = norm_back(grad_normed_two, scaled_two, inverse_two, gain_two)
    grad_hidden = grad_outside + back_two
    grad_mixer = grad_hidden.astype(jnp.bfloat16)
    out_proj_grad = dot_left(gated, grad_mixer)
    grad_gated = dot_right(grad_mixer, out_full).astype(jnp.bfloat16).astype(jnp.float32)
    grad_out_factor = grad_gated * convolved
    grad_conv = grad_gated * out_factor
    masked_grad = grad_conv * kept_one
    head_rows = jnp.stack([masked_grad[0], masked_grad[1] * kept_one[0, 0]])
    after = passed_along(head_rows, "seq", -1)
    next_grad = jnp.concatenate([masked_grad[1:], after[:1]], axis=0)
    folded = next_grad * kept_one
    later = jnp.concatenate([folded[1:], after[1:2]], axis=0)
    grad_product = taps[0] * grad_conv + taps[1] * next_grad + taps[2] * later
    tap_grads = jnp.stack(
        [
            jnp.sum(grad_conv * product, axis=0),
            jnp.sum(grad_conv * masked_prev, axis=0),
            jnp.sum(grad_conv * kept_one * older, axis=0),
        ]
    )
    grad_projected = jnp.stack(
        [grad_product * right_factor, grad_out_factor, grad_product * left_factor], axis=1
    ).astype(jnp.bfloat16)
    in_grad = jnp.einsum(
        "td,tkc->dkc", normed_one, grad_projected, preferred_element_type=jnp.float32
    )
    grad_normed_one = lax.psum(
        jnp.einsum("tkc,dkc->td", grad_projected, in_full, preferred_element_type=jnp.float32), "tp"
    )
    back_one, gain_one_grad = norm_back(grad_normed_one, scaled_one, inverse_one, gain_one)
    tokens_grad = grad_hidden + back_one
    gain_one_grad, gain_two_grad, tap_grads = lax.psum(
        (gain_one_grad, gain_two_grad, tap_grads), "seq"
    )
    in_grad, out_proj_grad, gate_grad, up_grad, down_grad = (
        lax.psum_scatter(in_grad, "seq", scatter_dimension=0, tiled=True),
        lax.psum_scatter(out_proj_grad, "seq", scatter_dimension=1, tiled=True),
        lax.psum_scatter(gate_grad, "seq", scatter_dimension=0, tiled=True),
        lax.psum_scatter(up_grad, "seq", scatter_dimension=0, tiled=True),
        lax.psum_scatter(down_grad, "seq", scatter_dimension=1, tiled=True),
    )
    return (
        result,
        tokens_grad,
        in_grad,
        tap_grads,
        out_proj_grad,
        gate_grad,
        up_grad,
        down_grad,
        gain_one_grad,
        gain_two_grad,
    )


def solution(mesh):
    in_specs = (
        P("seq", None),
        P("seq"),
        P(),
        P("seq", None, "tp"),
        P(None, "tp"),
        P("tp", "seq"),
        P(),
        P("seq", "tp"),
        P("seq", "tp"),
        P("tp", "seq"),
        P("seq", None),
    )
    out_specs = (
        P("seq", None),
        P("seq", None),
        P("seq", None, "tp"),
        P(None, "tp"),
        P("tp", "seq"),
        P("seq", "tp"),
        P("seq", "tp"),
        P("tp", "seq"),
        P(),
        P(),
    )
    return jax.shard_map(local, mesh=mesh, in_specs=in_specs, out_specs=out_specs, check_vma=False)
```

profile of v0, /device:TPU:0, one launch (start us, length us, event | category | flops | bytes accessed | tf_op | source)
XLA Modules:
  0.0 2030.1 jit_solution(10508599408486475542)
XLA Ops:
  7.2 0.7 all-gather.6.cloned.1.call-update
  8.0 0.7 all-gather.8.cloned.1.call-update
  8.7 3.1 fusion.10
  11.9 0.6 fusion.46
  12.5 45.7 %all-gather.6.cloned.1.call-done = bf16[2048,3,512]{2,0,1:T(8,128)(2,1)} async-done(((bf16[256,3,512]{2,0,1:T(8,128)(2,1)}), bf16[2048,3,512]{2,0,1:T(8,128)(2,1)}) %all-gather.6.cloned.1.call-update) | async-done | bytes 6291472 | tf_op jit(solution)/shard_map/all_gather | solution.py:51
  58.2 10.5 convolution_convert_fusion
  69.1 0.7 fusion.44
  69.8 2.2 collective-permute-start
  72.0 0.7 collective-permute-done
  73.1 1.3 copy-done.6
  74.4 2.3 multiply_add_fusion.1
  76.7 11.6 all-gather.8.cloned.1.call-done
  88.3 8.0 fusion.39
  96.3 0.5 all-gather.10.cloned.1.call-update
  96.9 0.5 all-gather.12.cloned.1.call-update
  97.5 0.5 all-gather.14.cloned.1.call-update
  98.1 289.2 %all-reduce.6.cloned.1.call-done = f32[1024,2048]{1,0:T(8,128)} async-done(((f32[1024,2048]{1,0:T(8,128)}), f32[1024,2048]{1,0:T(8,128)}) %all-reduce.6.cloned.1.call-update) | async-done | bytes 8388624 | tf_op jit(solution)/shard_map/psum | solution.py:78
  387.3 5.7 multiply_reduce_fusion.2
  393.0 3.5 copy-done
  396.6 2.8 multiply_convert_fusion.3
  399.3 43.1 %all-gather.10.cloned.1.call-done = bf16[2048,2048]{1,0:T(8,128)(2,1)} async-done(((bf16[256,2048]{1,0:T(8,128)(2,1)}), bf16[2048,2048]{1,0:T(8,128)(2,1)}) %all-gather.10.cloned.1.call-update) | async-done | bytes 8388624 | tf_op jit(solution)/shard_map/all_gather | solution.py:53
  442.4 14.7 fusion.49
  457.1 41.5 %all-gather.12.cloned.1.call-done = bf16[2048,2048]{1,0:T(8,128)(2,1)} async-done(((bf16[256,2048]{1,0:T(8,128)(2,1)}), bf16[2048,2048]{1,0:T(8,128)(2,1)}) %all-gather.12.cloned.1.call-update) | async-done | bytes 8388624 | tf_op jit(solution)/shard_map/all_gather | solution.py:54
  498.6 14.4 fusion.50
  513.0 43.3 %all-gather.14.cloned.1.call-done = bf16[2048,2048]{1,0:T(8,128)(2,1)} async-done(((bf16[2048,256]{1,0:T(8,128)(2,1)}), bf16[2048,2048]{1,0:T(8,128)(2,1)}) %all-gather.14.cloned.1.call-update) | async-done | bytes 8388624 | tf_op jit(solution)/shard_map/all_gather | solution.py:55
  556.3 21.8 %multiply_convert_fusion = (bf16[1024,2048]{1,0:T(8,128)(2,1)}, bf16[1024,2048]{1,0:T(8,128)(2,1)}, bf16[1024,2048]{1,0:T(8,128)(2,1)}) fusion(f32[1024,2048]{1,0:T(8,128)} %fusion.49, f32[1024,2048]{1,0:T(8,128)} %fusion.50, bf16[1024,2048]{1,0:T(8,128)(2,1)} %param.21, bf16[2048,2048]{1,0:T(8,128)(2,1)} %all-gather.14.cloned.1.call-done), kind=kOutput, calls=%fused_computation.17 | convolution fusion | flops 8621391872 | bytes 41943040 | tf_op jit(solution)/shard_map/dot_general | solution.py:20
  578.2 15.1 fusion.52
  593.3 13.0 convolution_add_fusion
  606.4 290.9 %all-reduce.8.cloned.1.call-done = f32[1024,2048]{1,0:T(8,128)} async-done(((f32[1024,2048]{1,0:T(8,128)}), f32[1024,2048]{1,0:T(8,128)}) %all-reduce.8.cloned.1.call-update) | async-done | bytes 8388624 | tf_op jit(solution)/shard_map/psum | solution.py:96
  897.3 7.6 multiply_reduce_fusion
  904.9 0.6 copy-done.4
  905.5 1.2 copy-done.8
  906.7 4.7 multiply_add_fusion
  911.5 2.4 fusion.30
  913.8 1.8 copy-done.1
  915.7 1.0 copy-done.5
  916.7 0.6 copy-done.7
  917.3 2.3 multiply_reduce_fusion.5
  919.6 0.7 fusion.43
  920.3 1.3 collective-permute-start.1
  921.6 13.4 fusion.51
  935.3 0.3 fusion.24
  935.7 1.0 fusion.34
  936.7 0.4 fusion.33
  937.1 0.5 copy-done.12
  937.6 0.4 copy-done.14
  938.1 0.5 slice-done.1
  938.5 8.9 convolution_bitcast_fusion
  947.5 8.5 fusion.25
  956.0 15.4 fusion.53
  971.5 15.3 fusion.54
  987.0 15.5 fusion.55
  1002.5 1.1 copy-done.11
  1003.6 0.3 copy-done.13
  1004.3 12.3 fusion.13
  1016.6 494.0 %all-reduce.10.cloned.1.call-done = (f32[1024,2048]{1,0:T(8,128)}, f32[1024,2048]{1,0:T(8,128)}) async-done(((f32[1024,2048]{1,0:T(8,128)}, f32[1024,2048]{1,0:T(8,128)}), (f32[1024,2048]{1,0:T(8,128)}, f32[1024,2048]{1,0:T(8,128)})) %all-reduce.10.cloned.1.call-update) | async-done | bytes 16777232 | tf_op jit(solution)/shard_map/psum | solution.py:88
  1510.6 5.8 fusion.9
  1516.5 24.8 %all-reduce = (f32[3,512]{1,0:T(4,128)}, f32[2048]{0:T(1024)}, f32[2048]{0:T(1024)}) all-reduce(f32[3,512]{1,0:T(4,128)S(1)} %pad_maximum_fusion.5, f32[2048]{0:T(1024)S(1)} %get-tuple-element.12, f32[2048]{0:T(1024)S(1)} %copy-done.20), channel_id=1, replica_groups=mesh['seq'=8,'tp'=4] {'seq'}, use_global_device_ids=true, to_apply=%region_12.0 | all-reduce | flops 5632 | bytes 45056 | tf_op jit(solution)/shard_map/psum | solution.py:130
  1541.3 20.1 fusion.8
  1561.4 3.5 reduce-scatter.8.cloned.1.call-done
  1564.9 120.4 %reduce-scatter.10.cloned.1.call-done = f32[256,2048]{1,0:T(8,128)} async-done(((f32[2048,2048]{1,0:T(8,128)}), f32[256,2048]{1,0:T(8,128)}) %reduce-scatter.10.cloned.1.call-update) | async-done | bytes 2097168 | tf_op jit(solution)/shard_map/reduce_scatter | solution.py:136
  1685.3 120.6 %reduce-scatter.12.cloned.1.call-done = f32[256,2048]{1,0:T(8,128)} async-done(((f32[2048,2048]{1,0:T(8,128)}), f32[256,2048]{1,0:T(8,128)}) %reduce-scatter.12.cloned.1.call-update) | async-done | bytes 2097168 | tf_op jit(solution)/shard_map/reduce_scatter | solution.py:137
  1805.9 120.4 %reduce-scatter.14.cloned.1.call-done = f32[2048,256]{1,0:T(8,128)} async-done(((f32[2048,2048]{1,0:T(8,128)}), f32[2048,256]{1,0:T(8,128)}) %reduce-scatter.14.cloned.1.call-update) | async-done | bytes 2097168 | tf_op jit(solution)/shard_map/reduce_scatter | solution.py:138
  1926.3 96.9 %reduce-scatter.6.cloned.1.call-done = f32[256,3,512]{2,0,1:T(8,128)} async-done(((f32[2048,3,512]{2,0,1:T(8,128)}), f32[256,3,512]{2,0,1:T(8,128)}) %reduce-scatter.6.cloned.1.call-update) | async-done | bytes 1572880 | tf_op jit(solution)/shard_map/reduce_scatter | solution.py:134
  (100 shorter events, 2.2 us)
Async XLA Ops:
  7.2 4.6 copy-start.30
  7.2 4.7 copy-start.28
  7.2 51.0 %all-gather.6.cloned.1.call-start = ((), (), s32[]{:S(2)}) async-start(), calls=%async_computation.5 | async-start | bytes 7077888 | tf_op jit(solution)/shard_map/all_gather | solution.py:51
  7.9 80.4 %all-gather.8.cloned.1.call-start = ((), (), s32[]{:S(2)}) async-start(), calls=%async_computation.6 | async-start | bytes 2359296 | tf_op jit(solution)/shard_map/all_gather | solution.py:52
  8.7 378.6 %all-reduce.6.cloned.1.call-start = ((), (), s32[]{:S(2)}) async-start(), calls=%async_computation.7 | async-start | bytes 16777216 | tf_op jit(solution)/shard_map/psum | solution.py:78
  11.8 56.9 %copy-start.18 = (f32[1024]{0:T(1024)}, f32[1024]{0:T(1024)S(1)}, u32[]{:S(2)}) copy-start(f32[1024]{0:T(1024)S(1)} %add_rsqrt_fusion.1) | copy-start | bytes 12292
  11.9 56.9 %copy-start.16 = (f32[2048]{0:T(1024)}, f32[2048]{0:T(1024)S(1)}, u32[]{:S(2)}) copy-start(f32[2048]{0:T(1024)S(1)} %convert_element_type.71) | copy-start | bytes 24580
  68.7 3.2 copy-start.27
  69.1 4.0 copy-start.2
  69.8 3.0 collective-permute-start
  72.0 1.1 copy-start.23
  72.0 1.1 copy-start.25
  72.0 4.7 copy-start.21
  73.0 1.3 copy-start.6
  96.3 1.8 copy-start.29
  96.3 346.2 %all-gather.10.cloned.1.call-start = ((), (), s32[]{:S(2)}) async-start(), calls=%async_computation.8 | async-start | bytes 9437184 | tf_op jit(solution)/shard_map/all_gather | solution.py:53
  96.9 401.7 %all-gather.12.cloned.1.call-start = ((), (), s32[]{:S(2)}) async-start(), calls=%async_computation.9 | async-start | bytes 9437184 | tf_op jit(solution)/shard_map/all_gather | solution.py:54
  97.5 458.9 %all-gather.14.cloned.1.call-start = ((), (), s32[]{:S(2)}) async-start(), calls=%async_computation.10 | async-start | bytes 9437184 | tf_op jit(solution)/shard_map/all_gather | solution.py:55
  98.0 799.2 %all-reduce.8.cloned.1.call-start = ((), (), s32[]{:S(2)}) async-start(), calls=%async_computation.11 | async-start | bytes 16777216 | tf_op jit(solution)/shard_map/psum | solution.py:96
  393.0 3.6 copy-start
  578.2 15.1 copy-start.31
  578.2 15.1 copy-start.32
  606.3 904.4 %all-reduce.10.cloned.1.call-start = ((), (), s32[]{:S(2)}) async-start(), calls=%async_computation.17 | async-start | bytes 33554432 | tf_op jit(solution)/shard_map/psum | solution.py:88
  897.3 8.2 copy-start.4
  897.3 9.4 copy-start.8
  906.7 4.7 copy-start.9
  911.4 4.3 copy-start.1
  911.4 4.2 copy-start.3
  911.4 5.2 copy-start.5
  911.4 5.9 copy-start.7
  917.3 4.3 copy-start.33
  919.6 17.5 copy-start.10
  920.3 14.9 collective-permute-start.1
  935.0 0.7 copy-start.22
  935.0 0.7 copy-start.24
  935.0 0.7 copy-start.26
  935.0 3.1 slice-start
  935.7 2.9 slice-start.1
  936.6 1.0 copy-start.12
  937.1 1.0 copy-start.14
  947.4 617.5 %reduce-scatter.8.cloned.1.call-start = ((), (), s32[]{:S(2)}) async-start(), calls=%async_computation.13 | async-start | bytes 4718592 | tf_op jit(solution)/shard_map/reduce_scatter | solution.py:135
  956.0 729.3 %reduce-scatter.10.cloned.1.call-start = ((), (), s32[]{:S(2)}) async-start(), calls=%async_computation.14 | async-start | bytes 18874368 | tf_op jit(solution)/shard_map/reduce_scatter | solution.py:136
  971.5 834.4 %reduce-scatter.12.cloned.1.call-start = ((), (), s32[]{:S(2)}) async-start(), calls=%async_computation.15 | async-start | bytes 18874368 | tf_op jit(solution)/shard_map/reduce_scatter | solution.py:137
  986.9 939.4 %reduce-scatter.14.cloned.1.call-start = ((), (), s32[]{:S(2)}) async-start(), calls=%async_computation.16 | async-start | bytes 18874368 | tf_op jit(solution)/shard_map/reduce_scatter | solution.py:138
  1002.4 1.2 copy-start.11
  1002.4 1.5 copy-start.13
  1002.4 1.9 copy-start.15
  1002.4 1.9 copy-start.17
  1002.4 1.8 copy-start.19
  1002.5 1020.7 %reduce-scatter.6.cloned.1.call-start = ((), (), s32[]{:S(2)}) async-start(), calls=%async_computation.12 | async-start | bytes 14155776 | tf_op jit(solution)/shard_map/reduce_scatter | solution.py:134
  1510.6 5.8 copy-start.20
Sparse Core Ops, SparseCore 0:
  9.9 48.2 all-gather.5
  60.1 28.1 all-gather.7
  96.4 290.8 all-reduce.5
  389.0 53.3 all-gather.9
  444.2 54.3 all-gather.11
  500.3 55.9 all-gather.13
  606.4 290.8 all-reduce.7
  947.5 563.0 all-reduce.9
  1514.6 50.2 reduce-scatter.7
  1569.3 115.9 reduce-scatter.9
  1689.9 115.9 reduce-scatter.11
  1810.3 115.9 reduce-scatter.13
  1930.7 92.3 reduce-scatter.5
where the time goes:
time: 2040 us; the launch traced here: 2030 us
  waiting for transfers between devices  1720 us (84%)
  matrix products  189 us (9%)
  other arithmetic  58.1 us (3%)
  blocking collectives  24.8 us (1%)
    psum x1, waiting for transfers between devices, local(): lax.psum(jnp.dot(activated, down_full, preferred_element_type=jnp.float32...  494 us
    psum x1, waiting for transfers between devices, local(): lax.psum(dot_right(grad_gate, gate_full) + dot_right(grad_up, up_full), '...  291 us
    psum x1, waiting for transfers between devices, local(): lax.psum(jnp.dot(gated, out_full, preferred_element_type=jnp.float32), 'tp')  289 us
    reduce_scatter x1, waiting for transfers between devices, local(): lax.psum_scatter(up_grad, 'seq', scatter_dimension=0, tiled=True)  121 us
    reduce_scatter x1, waiting for transfers between devices, local(): lax.psum_scatter(down_grad, 'seq', scatter_dimension=1, tiled=True)  120 us
    reduce_scatter x1, waiting for transfers between devices, local(): lax.psum_scatter(gate_grad, 'seq', scatter_dimension=0, tiled=True)  120 us
    reduce_scatter x1, waiting for transfers between devices, local(): lax.psum_scatter(in_grad, 'seq', scatter_dimension=0, tiled=True)  96.9 us
    dot_general x4, matrix products, dot_left(): lax.dot_general(left, right, (((0,), (0,)), ((), ())), preferred_element_...  54.7 us
  transfers between devices with their start and end apart: 15, of which 14 were waited for; matrix products, arithmetic and copies ran while one was open for 8% of the time, Pallas kernels for 0%

commit v1 on v0

--- a/solution.py
+++ b/solution.py
@@ -32,6 +32,15 @@
     weighted = grad_normed * gain
     back = inverse * (weighted - scaled * jnp.mean(weighted * scaled, axis=1, keepdims=True))
     return (back, jnp.sum(grad_normed * scaled, axis=0))
+
+
+def tp_sum(part):
+    return lax.psum(part.astype(jnp.bfloat16), "tp").astype(jnp.float32)
+
+
+def seq_scatter(part, dim):
+    narrow = part.astype(jnp.bfloat16)
+    return lax.psum_scatter(narrow, "seq", scatter_dimension=dim, tiled=True).astype(jnp.float32)
 
 
 def local(
@@ -75,7 +84,7 @@
     older = jnp.concatenate([before[1:2], masked_prev[:-1]], axis=0)
     convolved = taps[0] * product + taps[1] * masked_prev + taps[2] * kept_one * older
     gated = (out_factor * convolved).astype(jnp.bfloat16)
-    hidden = tokens_f + lax.psum(jnp.dot(gated, out_full, preferred_element_type=jnp.float32), "tp")
+    hidden = tokens_f + tp_sum(jnp.dot(gated, out_full, preferred_element_type=jnp.float32))
     inverse_two = rms_scale(hidden)
     scaled_two = hidden * inverse_two
     gain_two = norm_second.astype(jnp.float32)
@@ -85,7 +94,7 @@
     sigma = jax.nn.sigmoid(gate_val)
     swish = gate_val * sigma
     activated = (swish * up_val).astype(jnp.bfloat16)
-    ffn_out = lax.psum(jnp.dot(activated, down_full, preferred_element_type=jnp.float32), "tp")
+    ffn_out = tp_sum(jnp.dot(activated, down_full, preferred_element_type=jnp.float32))
     result = (hidden + ffn_out).astype(jnp.bfloat16)
     grad_act = dot_right(out_grad, down_full)
     down_grad = dot_left(activated, out_grad)
@@ -93,7 +102,7 @@
     grad_up = (grad_act * swish).astype(jnp.bfloat16)
     gate_grad = dot_left(normed_two, grad_gate)
     up_grad = dot_left(normed_two, grad_up)
-    grad_normed_two = lax.psum(dot_right(grad_gate, gate_full) + dot_right(grad_up, up_full), "tp")
+    grad_normed_two = tp_sum(dot_right(grad_gate, gate_full) + dot_right(grad_up, up_full))
     grad_outside = out_grad.astype(jnp.float32)
     back_two, gain_two_grad = norm_back(grad_normed_two, scaled_two, inverse_two, gain_two)
     grad_hidden = grad_outside + back_two
@@ -122,8 +131,8 @@
     in_grad = jnp.einsum(
         "td,tkc->dkc", normed_one, grad_projected, preferred_element_type=jnp.float32
     )
-    grad_normed_one = lax.psum(
-        jnp.einsum("tkc,dkc->td", grad_projected, in_full, preferred_element_type=jnp.float32), "tp"
+    grad_normed_one = tp_sum(
+        jnp.einsum("tkc,dkc->td", grad_projected, in_full, preferred_element_type=jnp.float32)
     )
     back_one, gain_one_grad = norm_back(grad_normed_one, scaled_one, inverse_one, gain_one)
     tokens_grad = grad_hidden + back_one
@@ -131,11 +140,11 @@
         (gain_one_grad, gain_two_grad, tap_grads), "seq"
     )
     in_grad, out_proj_grad, gate_grad, up_grad, down_grad = (
-        lax.psum_scatter(in_grad, "seq", scatter_dimension=0, tiled=True),
-        lax.psum_scatter(out_proj_grad, "seq", scatter_dimension=1, tiled=True),
-        lax.psum_scatter(gate_grad, "seq", scatter_dimension=0, tiled=True),
-        lax.psum_scatter(up_grad, "seq", scatter_dimension=0, tiled=True),
-        lax.psum_scatter(down_grad, "seq", scatter_dimension=1, tiled=True),
+        seq_scatter(in_grad, 0),
+        seq_scatter(out_proj_grad, 1),
+        seq_scatter(gate_grad, 0),
+        seq_scatter(up_grad, 0),
+        seq_scatter(down_grad, 1),
     )
     return (
         result,

time: 2040 us -> 1290 us (0.63)
  waiting for transfers between devices: 1720 us -> 976 us
    psum x3, waiting for transfers between devices: 1070 us -> 600 us  [tp_sum(): return lax.psum(part.astype(jnp.bfloat16), 'tp').astype(jnp.float32)]
    reduce_scatter x5, waiting for transfers between devices: 462 us -> 184 us  [seq_scatter(): lax.psum_scatter(narrow, 'seq', scatter_dimension=dim, tiled=True)]
  transfers between devices with their start and end apart: 15 -> 15, of which waited for: 14 -> 13; matrix products, arithmetic and copies ran while one was open for 8% -> 13% of each run, Pallas kernels for 0% -> 0%
where the time goes in v1:
time: 1290 us; the launch traced here: 1280 us
  waiting for transfers between devices  976 us (76%)
  matrix products  182 us (14%)
  other arithmetic  66.6 us (5%)
  blocking collectives  24.7 us (2%)
  between operations  14.7 us (1%)
    psum x3, waiting for transfers between devices, tp_sum(): return lax.psum(part.astype(jnp.bfloat16), 'tp').astype(jnp.float32)  600 us
    reduce_scatter x5, waiting for transfers between devices, seq_scatter(): lax.psum_scatter(narrow, 'seq', scatter_dimension=dim, tiled=True)  184 us
    dot_general x4, matrix products, dot_right(): lax.dot_general(left, right, (((1,), (1,)), ((), ())), preferred_element_...  55.3 us
    dot_general x4, matrix products, dot_left(): lax.dot_general(left, right, (((0,), (0,)), ((), ())), preferred_element_...  46.6 us
    all_gather x1, waiting for transfers between devices, local(): lax.all_gather(in_weight, 'seq', axis=0, tiled=True)  45.7 us
    all_gather x1, waiting for transfers between devices, local(): lax.all_gather(gate_weight, 'seq', axis=0, tiled=True)  45.4 us
    all_gather x1, waiting for transfers between devices, local(): lax.all_gather(down_weight, 'seq', axis=1, tiled=True)  43.4 us
    all_gather x1, waiting for transfers between devices, local(): lax.all_gather(up_weight, 'seq', axis=0, tiled=True)  41.8 us
  transfers between devices with their start and end apart: 15, of which 13 were waited for; matrix products, arithmetic and copies ran while one was open for 13% of the time, Pallas kernels for 0%

profile of v1, /device:TPU:0, one launch (start us, length us, event | category | flops | bytes accessed | tf_op | source)
XLA Modules:
  0.0 1279.4 jit_solution(4072105731136228841)
XLA Ops:
  7.2 0.7 all-gather.6.cloned.1.call-update
  8.0 0.7 all-gather.8.cloned.1.call-update
  8.7 3.1 fusion.16
  11.9 0.6 fusion.50
  12.5 45.7 %all-gather.6.cloned.1.call-done = bf16[2048,3,512]{2,0,1:T(8,128)(2,1)} async-done(((bf16[256,3,512]{2,0,1:T(8,128)(2,1)}), bf16[2048,3,512]{2,0,1:T(8,128)(2,1)}) %all-gather.6.cloned.1.call-update) | async-done | bytes 6291472 | tf_op jit(solution)/shard_map/all_gather | solution.py:60
  58.2 10.5 convolution_convert_fusion.7
  69.1 0.7 fusion.48
  69.8 2.2 collective-permute-start
  72.0 0.8 collective-permute-done
  73.3 1.0 copy-done.7
  74.4 2.3 multiply_add_fusion
  76.7 11.6 all-gather.8.cloned.1.call-done
  88.3 6.6 convolution_convert_fusion.5
  95.0 0.5 all-gather.10.cloned.1.call-update
  95.5 0.5 all-gather.12.cloned.1.call-update
  96.1 0.5 all-gather.14.cloned.1.call-update
  96.6 0.6 all-reduce.8.cloned.1.call-start
  97.2 152.8 %all-reduce.6.cloned.1.call-done = bf16[1024,2048]{1,0:T(8,128)(2,1)} async-done(((bf16[1024,2048]{1,0:T(8,128)(2,1)}), bf16[1024,2048]{1,0:T(8,128)(2,1)}) %all-reduce.6.cloned.1.call-update) | async-done | bytes 4194320 | tf_op jit(solution)/shard_map/psum | solution.py:38
  250.0 5.0 multiply_reduce_fusion
  255.1 0.9 copy-done.2
  255.9 4.0 multiply_convert_fusion.3
  260.0 45.4 %all-gather.10.cloned.1.call-done = bf16[2048,2048]{1,0:T(8,128)(2,1)} async-done(((bf16[256,2048]{1,0:T(8,128)(2,1)}), bf16[2048,2048]{1,0:T(8,128)(2,1)}) %all-gather.10.cloned.1.call-update) | async-done | bytes 8388624 | tf_op jit(solution)/shard_map/all_gather | solution.py:62
  305.4 14.5 %fusion.53 = f32[1024,2048]{1,0:T(8,128)} fusion(bf16[1024,2048]{1,0:T(8,128)(2,1)} %multiply_convert_fusion.3, bf16[2048,2048]{1,0:T(8,128)(2,1)} %all-gather.10.cloned.1.call-done), kind=kOutput, calls=%fused_computation.97 | convolution fusion | flops 8589934592 | bytes 20971520 | tf_op jit(solution)/shard_map/dot_general | solution.py:92
  319.8 41.8 %all-gather.12.cloned.1.call-done = bf16[2048,2048]{1,0:T(8,128)(2,1)} async-done(((bf16[256,2048]{1,0:T(8,128)(2,1)}), bf16[2048,2048]{1,0:T(8,128)(2,1)}) %all-gather.12.cloned.1.call-update) | async-done | bytes 8388624 | tf_op jit(solution)/shard_map/all_gather | solution.py:63
  361.7 14.4 %fusion.54 = f32[1024,2048]{1,0:T(8,128)} fusion(bf16[1024,2048]{1,0:T(8,128)(2,1)} %multiply_convert_fusion.3, bf16[2048,2048]{1,0:T(8,128)(2,1)} %all-gather.12.cloned.1.call-done), kind=kOutput, calls=%fused_computation.98 | convolution fusion | flops 8589934592 | bytes 20971520 | tf_op jit(solution)/shard_map/dot_general | solution.py:93
  376.1 43.4 %all-gather.14.cloned.1.call-done = bf16[2048,2048]{1,0:T(8,128)(2,1)} async-done(((bf16[2048,256]{1,0:T(8,128)(2,1)}), bf16[2048,2048]{1,0:T(8,128)(2,1)}) %all-gather.14.cloned.1.call-update) | async-done | bytes 8388624 | tf_op jit(solution)/shard_map/all_gather | solution.py:64
  419.6 22.0 %multiply_convert_fusion = (bf16[1024,2048]{1,0:T(8,128)(2,1)}, bf16[1024,2048]{1,0:T(8,128)(2,1)}, bf16[1024,2048]{1,0:T(8,128)(2,1)}) fusion(f32[1024,2048]{1,0:T(8,128)} %fusion.53, f32[1024,2048]{1,0:T(8,128)} %fusion.54, bf16[1024,2048]{1,0:T(8,128)(2,1)} %param.21, bf16[2048,2048]{1,0:T(8,128)(2,1)} %all-gather.14.cloned.1.call-done), kind=kOutput, calls=%fused_computation.25 | convolution fusion | flops 8621391872 | bytes 41943040 | tf_op jit(solution)/shard_map/dot_general | solution.py:20
  441.5 14.7 %fusion.55 = f32[1024,2048]{1,0:T(8,128)} fusion(bf16[1024,2048]{1,0:T(8,128)(2,1)} %get-tuple-element.26, bf16[2048,2048]{1,0:T(8,128)(2,1)} %all-gather.10.cloned.1.call-done), kind=kOutput, calls=%fused_computation.99 | convolution fusion | flops 8589934592 | bytes 20971520 | tf_op jit(solution)/shard_map/dot_general | solution.py:20
  456.2 12.2 add_convert_fusion
  468.5 155.1 %all-reduce.8.cloned.1.call-done = bf16[1024,2048]{1,0:T(8,128)(2,1)} async-done(((bf16[1024,2048]{1,0:T(8,128)(2,1)}), bf16[1024,2048]{1,0:T(8,128)(2,1)}) %all-reduce.8.cloned.1.call-update) | async-done | bytes 4194320 | tf_op jit(solution)/shard_map/psum | solution.py:38
  623.6 7.9 fusion.12
  631.9 6.8 fusion.11
  638.7 3.4 copy-done.6
  642.1 3.9 convolution_convert_fusion.6
  646.1 14.0 %convolution_convert_fusion.2 = bf16[2048,2048]{1,0:T(8,128)(2,1)} fusion(bf16[1024,2048]{1,0:T(8,128)(2,1)} %multiply_convert_fusion.3, bf16[1024,2048]{1,0:T(8,128)(2,1)} %get-tuple-element.26), kind=kOutput, calls=%fused_computation.35 | convolution fusion | flops 8594128896 | bytes 16777216 | tf_op jit(solution)/shard_map/dot_general | solution.py:26
  660.2 14.5 %convolution_convert_fusion.1 = bf16[2048,2048]{1,0:T(8,128)(2,1)} fusion(bf16[1024,2048]{1,0:T(8,128)(2,1)} %multiply_convert_fusion.3, bf16[1024,2048]{1,0:T(8,128)(2,1)} %get-tuple-element.25), kind=kOutput, calls=%fused_computation.34 | convolution fusion | flops 8594128896 | bytes 16777216 | tf_op jit(solution)/shard_map/dot_general | solution.py:26
  674.8 14.1 %convolution_convert_fusion = bf16[2048,2048]{1,0:T(8,128)(2,1)} fusion(bf16[1024,2048]{1,0:T(8,128)(2,1)} %get-tuple-element.27, bf16[1024,2048]{1,0:T(8,128)(2,1)} %param.21), kind=kOutput, calls=%fused_computation.33 | convolution fusion | flops 8594128896 | bytes 16777216 | tf_op jit(solution)/shard_map/dot_general | solution.py:26
  689.0 0.6 copy-done.19
  689.7 6.5 fusion.35
  696.2 2.5 multiply_reduce_fusion.3
  698.8 0.6 fusion.47
  699.3 1.3 collective-permute-start.1
  700.6 13.3 %convolution_convert_fusion.4 = bf16[1024,2048]{1,0:T(8,128)(2,1)} fusion(bf16[1024,2048]{1,0:T(8,128)(2,1)S(1)} %copy-done.40, bf16[2048,2048]{1,0:T(8,128)(2,1)} %all-gather.14.cloned.1.call-done), kind=kOutput, calls=%fused_computation.39 | convolution fusion | flops 8592031744 | bytes 16777216 | tf_op jit(solution)/shard_map/dot_general | solution.py:97
  714.6 1.0 fusion.39
  716.1 0.5 copy-done.14
  716.6 0.5 copy-done.16
  717.1 1.1 slice-done.1
  718.2 8.2 bitcast_convert_fusion
  726.5 1.1 copy-done.13
  728.1 0.5 copy-done.17
  728.5 12.1 convolution_convert_fusion.3
  740.6 1.8 convert_element_type.158
  742.4 19.2 %reduce-scatter.10.cloned.1.call-done = bf16[256,2048]{1,0:T(8,128)(2,1)} async-done(((bf16[2048,2048]{1,0:T(8,128)(2,1)}), bf16[256,2048]{1,0:T(8,128)(2,1)}) %reduce-scatter.10.cloned.1.call-update) | async-done | bytes 1048592 | tf_op jit(solution)/shard_map/reduce_scatter | solution.py:43
  761.7 2.8 convert_element_type.160
  764.4 71.8 %reduce-scatter.12.cloned.1.call-done = bf16[256,2048]{1,0:T(8,128)(2,1)} async-done(((bf16[2048,2048]{1,0:T(8,128)(2,1)}), bf16[256,2048]{1,0:T(8,128)(2,1)}) %reduce-scatter.12.cloned.1.call-update) | async-done | bytes 1048592 | tf_op jit(solution)/shard_map/reduce_scatter | solution.py:43
  836.2 2.8 convert_element_type.162
  839.0 72.4 %reduce-scatter.14.cloned.1.call-done = bf16[2048,256]{1,0:T(8,128)(2,1)} async-done(((bf16[2048,2048]{1,0:T(8,128)(2,1)}), bf16[2048,256]{1,0:T(8,128)(2,1)}) %reduce-scatter.14.cloned.1.call-update) | async-done | bytes 1048592 | tf_op jit(solution)/shard_map/reduce_scatter | solution.py:43
  911.4 2.7 convert_element_type.164
  914.1 291.9 %all-reduce.10.cloned.1.call-done = (bf16[1024,2048]{1,0:T(8,128)(2,1)}, bf16[1024,2048]{1,0:T(8,128)(2,1)}) async-done(((bf16[1024,2048]{1,0:T(8,128)(2,1)}, bf16[1024,2048]{1,0:T(8,128)(2,1)}), (bf16[1024,2048]{1,0:T(8,128)(2,1)}, bf16[1024,2048]{1,0:T(8,128)(2,1)})) %all-reduce.10.cloned.1.call-update) | async-done | bytes 8388624 | tf_op jit(solution)/shard_map/psum | solution.py:38
  1206.0 5.0 fusion.15
  1211.0 24.7 %all-reduce = (f32[3,512]{1,0:T(4,128)}, f32[2048]{0:T(1024)}, f32[2048]{0:T(1024)}) all-reduce(f32[3,512]{1,0:T(4,128)S(1)} %pad_maximum_fusion.5, f32[2048]{0:T(1024)S(1)} %get-tuple-element.12, f32[2048]{0:T(1024)S(1)} %get-tuple-element.10), channel_id=1, replica_groups=mesh['seq'=8,'tp'=4] {'seq'}, use_global_device_ids=true, to_apply=%region_12.0 | all-reduce | flops 5632 | bytes 45056 | tf_op jit(solution)/shard_map/psum | solution.py:139
  1235.7 13.9 %fusion.8 = (f32[1024,2048]{1,0:T(8,128)}, bf16[1024,2048]{1,0:T(8,128)(2,1)}) fusion(f32[1024,2048]{1,0:T(8,128)} %copy-done.6, bf16[1024,2048]{1,0:T(8,128)(2,1)} %get-tuple-element.20, bf16[1024,2048]{1,0:T(8,128)(2,1)} %param.11, f32[1024]{0:T(1024)S(1)} %broadcast_multiply_fusion, f32[2048]{0:T(1024)S(1)} %copy-done.21, f32[1024]{0:T(1024)S(1)} %copy-done.23, ...), kind=kLoop, calls=%fused_computation.14 | loop fusion | flops 27262976 | bytes 37765120 | tf_op jit(solution)/shard_map/add | solution.py:138
  1249.6 20.6 %reduce-scatter.6.cloned.1.call-done = bf16[256,3,512]{2,0,1:T(8,128)(2,1)} async-done(((bf16[2048,3,512]{2,0,1:T(8,128)(2,1)}), bf16[256,3,512]{2,0,1:T(8,128)(2,1)}) %reduce-scatter.6.cloned.1.call-update) | async-done | bytes 786448 | tf_op jit(solution)/shard_map/reduce_scatter | solution.py:43
  1270.2 2.5 convert_element_type.156
  (119 shorter events, 3.7 us)
Async XLA Ops:
  7.2 4.6 copy-start.37
  7.2 4.7 copy-start.35
  7.2 51.0 %all-gather.6.cloned.1.call-start = ((), (), s32[]{:S(2)}) async-start(), calls=%async_computation.5 | async-start | bytes 7077888 | tf_op jit(solution)/shard_map/all_gather | solution.py:60
  7.9 80.4 %all-gather.8.cloned.1.call-start = ((), (), s32[]{:S(2)}) async-start(), calls=%async_computation.6 | async-start | bytes 2359296 | tf_op jit(solution)/shard_map/all_gather | solution.py:61
  8.7 241.3 %all-reduce.6.cloned.1.call-start = ((), (), s32[]{:S(2)}) async-start(), calls=%async_computation.7 | async-start | bytes 8388608 | tf_op jit(solution)/shard_map/psum | solution.py:38
  11.8 56.9 %copy-start.22 = (f32[1024]{0:T(1024)}, f32[1024]{0:T(1024)S(1)}, u32[]{:S(2)}) copy-start(f32[1024]{0:T(1024)S(1)} %add_rsqrt_fusion.1) | copy-start | bytes 12292
  11.9 61.2 %copy-start.18 = (f32[1024]{0:T(1024)}, f32[1024]{0:T(1024)S(1)}, u32[]{:S(2)}) copy-start(f32[1024]{0:T(1024)S(1)} %subtract_convert_fusion) | copy-start | bytes 12292
  11.9 56.9 %copy-start.20 = (f32[2048]{0:T(1024)}, f32[2048]{0:T(1024)S(1)}, u32[]{:S(2)}) copy-start(f32[2048]{0:T(1024)S(1)} %convert_element_type.125) | copy-start | bytes 24580
  68.7 3.2 copy-start.34
  69.1 4.0 copy-start.4
  69.8 3.0 collective-permute-start
  72.0 1.1 copy-start.26
  72.0 1.1 copy-start.28
  72.0 1.1 copy-start.30
  72.8 0.6 copy-start.24
  72.8 0.6 copy-start.32
  73.1 1.3 copy-start.7
  94.9 2.3 copy-start.36
  94.9 210.5 %all-gather.10.cloned.1.call-start = ((), (), s32[]{:S(2)}) async-start(), calls=%async_computation.8 | async-start | bytes 9437184 | tf_op jit(solution)/shard_map/all_gather | solution.py:62
  95.5 266.2 %all-gather.12.cloned.1.call-start = ((), (), s32[]{:S(2)}) async-start(), calls=%async_computation.9 | async-start | bytes 9437184 | tf_op jit(solution)/shard_map/all_gather | solution.py:63
  96.1 323.5 %all-gather.14.cloned.1.call-start = ((), (), s32[]{:S(2)}) async-start(), calls=%async_computation.10 | async-start | bytes 9437184 | tf_op jit(solution)/shard_map/all_gather | solution.py:64
  96.6 527.0 %all-reduce.8.cloned.1.call-start = ((), (), s32[]{:S(2)}) async-start(), calls=%async_computation.11 | async-start | bytes 8388608 | tf_op jit(solution)/shard_map/psum | solution.py:38
  250.0 5.0 copy-start
  250.0 5.9 copy-start.2
  441.5 14.7 %copy-start.38 = (bf16[2048,2048]{1,0:T(8,128)(2,1)S(1)}, bf16[2048,2048]{1,0:T(8,128)(2,1)}, u32[]{:S(2)}) copy-start(bf16[2048,2048]{1,0:T(8,128)(2,1)} %all-gather.12.cloned.1.call-done) | copy-start | bytes 25165828
  441.5 14.7 %copy-start.39 = (bf16[1024,2048]{1,0:T(8,128)(2,1)S(1)}, bf16[1024,2048]{1,0:T(8,128)(2,1)}, u32[]{:S(2)}) copy-start(bf16[1024,2048]{1,0:T(8,128)(2,1)} %get-tuple-element.25) | copy-start | bytes 12582916
  468.5 272.2 %reduce-scatter.8.cloned.1.call-start = ((), (), s32[]{:S(2)}) async-start(), calls=%async_computation.13 | async-start | bytes 2359296 | tf_op jit(solution)/shard_map/reduce_scatter | solution.py:43
  623.6 7.9 copy-start.1
  623.6 7.9 copy-start.3
  623.6 8.3 copy-start.9
  631.9 10.2 copy-start.10
  638.7 3.4 copy-start.6
  646.1 115.6 %reduce-scatter.10.cloned.1.call-start = ((), (), s32[]{:S(2)}) async-start(), calls=%async_computation.14 | async-start | bytes 9437184 | tf_op jit(solution)/shard_map/reduce_scatter | solution.py:43
  660.2 176.1 %reduce-scatter.12.cloned.1.call-start = ((), (), s32[]{:S(2)}) async-start(), calls=%async_computation.15 | async-start | bytes 9437184 | tf_op jit(solution)/shard_map/reduce_scatter | solution.py:43
  674.8 236.7 %reduce-scatter.14.cloned.1.call-start = ((), (), s32[]{:S(2)}) async-start(), calls=%async_computation.16 | async-start | bytes 9437184 | tf_op jit(solution)/shard_map/reduce_scatter | solution.py:43
  688.9 0.7 copy-start.19
  688.9 517.1 %all-reduce.10.cloned.1.call-start = ((), (), s32[]{:S(2)}) async-start(), calls=%async_computation.17 | async-start | bytes 16777216 | tf_op jit(solution)/shard_map/psum | solution.py:38
  689.7 6.5 copy-start.5
  689.7 6.5 copy-start.8
  689.7 6.5 copy-start.11
  689.7 6.5 copy-start.25
  689.7 6.5 copy-start.33
  696.2 4.4 copy-start.40
  698.7 17.3 %copy-start.12 = (bf16[1024,1,512]{2,0,1:T(8,128)(2,1)}, bf16[1024,1,512]{2,0,1:T(8,128)(2,1)S(1)}, u32[]{:S(2)}) copy-start(bf16[1024,1,512]{2,0,1:T(8,128)(2,1)S(1)} %get-tuple-element.36) | copy-start | bytes 3145732
  699.3 14.9 %collective-permute-start.1 = (f32[2,512]{1,0:T(2,128)S(1)}, f32[2,512]{1,0:T(2,128)S(1)}, u32[]{:S(2)}, u32[]{:S(2)}) collective-permute-start(f32[2,512]{1,0:T(2,128)S(1)} %pad_maximum_fusion.7), channel_id=1, source_target_pairs={{4,0},{8,4},{12,8},{16,12},{20,16},{24,20},{28,24},{5,1},{9,5},{13... | collective-permute-start | bytes 12296 | tf_op jit(solution)/shard_map/ppermute | solution.py:12
  713.9 0.7 copy-start.27
  713.9 0.7 copy-start.29
  713.9 0.7 copy-start.31
  713.9 3.2 slice-start
  714.6 3.5 slice-start.1
  715.6 1.0 copy-start.14
  716.1 1.0 copy-start.16
  726.4 1.2 copy-start.13
  726.4 1.7 copy-start.15
  726.4 2.1 copy-start.17
  726.4 2.1 copy-start.21
  726.4 2.1 copy-start.23
  726.4 543.7 %reduce-scatter.6.cloned.1.call-start = ((), (), s32[]{:S(2)}) async-start(), calls=%async_computation.12 | async-start | bytes 7077888 | tf_op jit(solution)/shard_map/reduce_scatter | solution.py:43
Sparse Core Ops, SparseCore 0:
  9.9 48.2 all-gather.5
  60.1 28.1 all-gather.7
  95.0 154.9 all-reduce.5
  251.9 53.3 all-gather.9
  307.3 54.3 all-gather.11
  363.6 55.9 all-gather.13
  468.6 154.9 all-reduce.7
  646.2 40.2 reduce-scatter.7
  690.3 71.3 reduce-scatter.9
  765.0 71.2 reduce-scatter.11
  840.1 71.2 reduce-scatter.13
  914.5 291.5 all-reduce.9
  1209.4 60.7 reduce-scatter.5
